TPU v7x, 32 devices: a whole 2x2x4 slice. The times are simulated.
32 devices in a mesh: grp: 2 (over y), row: 8 (over z, x), head: 2 (over core).
Axes of the slice: x: 2, y: 2, z: 4, core: 2. Of those that a mesh axis runs over, the one named last changes fastest.
Arguments:
- latent: bfloat16 [16, 256, 512], P(('grp', 'row')), parts along dimension 0, may hold values from -6 to 6
- weights: bfloat16 [512, 8, 512], P(None, None, 'head'), may hold values from -0.25 to 0.25
- cotangent: bfloat16 [16, 256, 512], P(('grp', 'row')), parts along dimension 0, may hold values from -6 to 6
Outputs:
- latent_grad: bfloat16 [16, 256, 512], P(('grp', 'row')), parts along dimension 0
- weight_grad: float32 [1024, 8, 512], P(('grp', 'row'), None, 'head'), parts along dimension 0
There are 2 independent parts, one for each index of `grp`. A program takes and returns all parts, laid end to end along the dimension named above; an argument that names none is the same for every part. Nothing has to cross between parts.
All inputs are finite; a program needn't handle non-finite values.
Results may differ from a plain program's by a relative error of at most 0.03.
Values may be sent and summed in bfloat16 or wider, within the bound.
A program may use at most 64 MiB of HBM per device.

v0:
```python
import math

import jax
import jax.numpy as jnp
from jax import lax
from jax.sharding import PartitionSpec as P

HEAD_DIM = 64


epsilon = 1e-06


def index_pair(pattern):
    return (pattern + "hd", pattern.replace("l", "m") + "hd")


def head_norm(values):
    inverse = lax.rsqrt(jnp.mean(values * values, axis=-1, keepdims=True) + epsilon)
    return (values * inverse, inverse)


def three_maps(weights, first):
    width = weights.shape[0]
    return weights[:, first : first + 3, :].reshape(width, 3 * weights.shape[2])


def attend_local(inputs, weights, first, pattern):
    outer, inner, width = inputs.shape
    local = weights.shape[2]
    heads_here = local // HEAD_DIM
    logit_scale = 2.0 / math.sqrt(HEAD_DIM)
    flat = inputs.reshape(outer * inner, width)
    joined = jnp.dot(flat, three_maps(weights, first), preferred_element_type=jnp.float32)
    shaped = joined.reshape(outer, inner, 3, heads_here, HEAD_DIM)
    query_n, query_r = head_norm(shaped[:, :, 0])
    key_n, key_r = head_norm(shaped[:, :, 1])
    query_batched = query_n.astype(jnp.bfloat16)
    key_batched = key_n.astype(jnp.bfloat16)
    value_batched = shaped[:, :, 2].astype(jnp.bfloat16)
    query_ix, key_ix = index_pair(pattern)
    attention_logits = logit_scale * jnp.einsum(
        query_ix + "," + key_ix + "->shlm",
        query_batched,
        key_batched,
        preferred_element_type=jnp.float32,
    )
    expo = jnp.exp(attention_logits)
    probs = expo / jnp.sum(expo, axis=-1, keepdims=True)
    probability_batched = probs.astype(jnp.bfloat16)
    attention_output = jnp.einsum(
        "shlm," + key_ix + "->" + query_ix,
        probability_batched,
        value_batched,
        preferred_element_type=jnp.float32,
    ).astype(jnp.bfloat16)
    saved = (
        query_n,
        query_r,
        query_batched,
        key_n,
        key_r,
        key_batched,
        value_batched,
        probs,
        probability_batched,
    )
    return (flat, saved, attention_output.reshape(outer * inner, local))


def attend_back(saved, upstream, weights, first, pattern):
    outer, inner, width = upstream.shape
    local = weights.shape[2]
    heads_here = local // HEAD_DIM
    logit_scale = 2.0 / math.sqrt(HEAD_DIM)
    (
        query_n,
        query_r,
        query_batched,
        key_n,
        key_r,
        key_batched,
        value_batched,
        probs,
        probability_batched,
    ) = saved
    query_ix, key_ix = index_pair(pattern)
    grad_flat = upstream.reshape(outer * inner, width)
    grad_att = jnp.dot(
        grad_flat, weights[:, first + 3, :], preferred_element_type=jnp.float32
    ).astype(jnp.bfloat16)
    grad_att = grad_att.reshape(outer, inner, heads_here, HEAD_DIM)
    gradient_value_rows = jnp.einsum(
        "shlm," + query_ix + "->" + key_ix,
        probability_batched,
        grad_att,
        preferred_element_type=jnp.float32,
    ).astype(jnp.bfloat16)
    gradient_probability = jnp.einsum(
        query_ix + "," + key_ix + "->shlm",
        grad_att,
        value_batched,
        preferred_element_type=jnp.float32,
    )
    delta = jnp.sum(probs * gradient_probability, axis=-1, keepdims=True)
    gradient_logits = (probs * (gradient_probability - delta)).astype(jnp.bfloat16)
    gradient_normed_query = logit_scale * jnp.einsum(
        "shlm," + key_ix + "->" + query_ix,
        gradient_logits,
        key_batched,
        preferred_element_type=jnp.float32,
    )
    gradient_normed_key = logit_scale * jnp.einsum(
        "shlm," + query_ix + "->" + key_ix,
        gradient_logits,
        query_batched,
        preferred_element_type=jnp.float32,
    )
    grad_query = (
        query_r
        * (
            gradient_normed_query
            - query_n * jnp.mean(gradient_normed_query * query_n, axis=-1, keepdims=True)
        )
    ).astype(jnp.bfloat16)
    grad_key = (
        key_r
        * (
            gradient_normed_key
            - key_n * jnp.mean(gradient_normed_key * key_n, axis=-1, keepdims=True)
        )
    ).astype(jnp.bfloat16)
    stacked = jnp.stack([grad_query, grad_key, gradient_value_rows], axis=2).reshape(
        outer * inner, 3 * local
    )
    partial_in = lax.dot_general(
        stacked,
        three_maps(weights, first),
        (((1,), (1,)), ((), ())),
        preferred_element_type=jnp.float32,
    )
    return (partial_in, stacked, grad_flat)


def weight_terms(flat, stacked, grad_flat, attention_output, count):
    contract = (((0,), (0,)), ((), ()))
    three = lax.dot_general(flat, stacked, contract, preferred_element_type=jnp.float32)
    last = lax.dot_general(
        grad_flat, attention_output, contract, preferred_element_type=jnp.float32
    )
    return jnp.concatenate((three.reshape(count, 3, -1), last.reshape(count, 1, -1)), 1)


def head_sum(partial_value):
    return lax.psum(partial_value.astype(jnp.bfloat16), "head").astype(jnp.float32)


def on_device(latent, weights, cotangent):
    rows, cols, width = latent.shape
    rows_here = width // lax.axis_size("row")
    flat_row, saved_row, attended_row = attend_local(latent, weights, 0, "sl")
    mixed = head_sum(
        lax.dot_general(
            attended_row,
            weights[:, 3, :],
            (((1,), (1,)), ((), ())),
            preferred_element_type=jnp.float32,
        )
    )
    first_out = (latent.astype(jnp.float32) + mixed.reshape(rows, cols, width)).astype(jnp.bfloat16)
    columns, cotangent_cols = (
        lax.all_to_all(first_out, "row", split_axis=1, concat_axis=0, tiled=True),
        lax.all_to_all(cotangent, "row", split_axis=1, concat_axis=0, tiled=True),
    )
    height = columns.shape[0]
    flat_col, saved_col, attended_col = attend_local(columns, weights, 4, "ls")
    partial_col, stacked_col, grad_col = attend_back(saved_col, cotangent_cols, weights, 4, "ls")
    grad_mid = (
        cotangent_cols.astype(jnp.float32) + head_sum(partial_col).reshape(columns.shape)
    ).astype(jnp.bfloat16)
    grad_first = lax.all_to_all(grad_mid, "row", split_axis=0, concat_axis=1, tiled=True)
    partial_row, stacked_row, grad_row = attend_back(saved_row, grad_first, weights, 0, "sl")
    latent_grad = (
        grad_first.astype(jnp.float32) + head_sum(partial_row).reshape(latent.shape)
    ).astype(jnp.bfloat16)
    summed = lax.psum_scatter(
        jnp.concatenate(
            (
                weight_terms(
                    flat_row, stacked_row, grad_row, attended_row, rows_here * lax.axis_size("row")
                ),
                weight_terms(
                    flat_col, stacked_col, grad_col, attended_col, rows_here * lax.axis_size("row")
                ),
            ),
            1,
        ),
        "row",
        scatter_dimension=0,
        tiled=True,
    )
    weight_grad = summed * (1.0 / math.sqrt(height * cols))
    return (latent_grad, weight_grad)


def solution(mesh):
    in_specs = (P(("grp", "row"), None, None), P(None, None, "head"), P(("grp", "row"), None, None))
    out_specs = (P(("grp", "row"), None, None), P(("grp", "row"), None, "head"))
    return jax.shard_map(
        on_device, mesh=mesh, in_specs=in_specs, out_specs=out_specs, check_vma=False
    )
```

profile of v0, /device:TPU:0, one launch (start us, length us, event | category | flops | bytes accessed | tf_op | source)
XLA Modules:
  0.0 247.7 jit_solution(1502684918247256493)
XLA Ops:
  7.2 4.4 %fusion.70 = (bf16[512,1,256]{2,1,0:T(2,128)(2,1)}, bf16[512,1,256]{2,1,0:T(2,128)(2,1)}) fusion(bf16[512,8,256]{2,1,0:T(8,128)(2,1)} %param.4), kind=kLoop, calls=%fused_computation.123 | loop fusion | bytes 1048576 | tf_op jit(solution)/shard_map/slice | solution.py:165
  11.7 0.7 fusion.69
  12.3 0.9 copy.132
  13.3 0.4 convolution_bitcast_fusion
  14.4 0.4 fusion.15
  15.1 0.8 copy-done.15
  15.9 1.0 fusion.2
  16.9 2.1 copy.187
  19.0 0.5 broadcast.179
  19.6 3.0 %reduce.8 = bf16[256,512]{1,0:T(8,128)(2,1)S(1)} reduce(bf16[256,1,512]{2,1,0:T(2,128)(2,1)} %bitcast.232, bf16[]{:T(256)} %broadcast.179), dimensions={1}, to_apply=%bitcast.221.reduce_sub_computation | reduce | bytes 524290
  22.6 0.9 reshape.315
  23.5 7.3 %all-to-all-start = ((bf16[8,2,8192]{2,1,0:T(2,128)(2,1)}), bf16[8,2,8192]{2,1,0:T(2,128)(2,1)}, u32[]{:S(2)}, u32[]{:S(2)}) async-start(bf16[8,2,8192]{2,1,0:T(2,128)(2,1)} %reshape.315), calls=%async_computation | async-start | bytes 524288 | tf_op jit(solution)/shard_map/all_to_all | solution.py:173
  30.7 7.3 %all-reduce.4.cloned.1.call-done = bf16[1,256,512]{2,1,0:T(8,128)(2,1)} async-done(((bf16[1,256,512]{2,1,0:T(8,128)(2,1)}), bf16[1,256,512]{2,1,0:T(8,128)(2,1)}) %all-reduce.4.cloned.1.call-update) | async-done | bytes 262160 | tf_op jit(solution)/shard_map/psum | solution.py:155
  38.0 1.0 add_convert_fusion.1
  39.0 0.4 copy.186
  39.4 2.8 %reduce.9 = bf16[256,512]{1,0:T(8,128)(2,1)} reduce(bf16[256,1,512]{2,1,0:T(2,128)(2,1)S(1)} %bitcast.233, bf16[]{:T(256)} %broadcast.179), dimensions={1}, to_apply=%bitcast.220.reduce_sub_computation | reduce | bytes 524290
  42.3 1.8 reshape.317
  44.1 5.8 %all-to-all-start.1 = ((bf16[8,2,8192]{2,1,0:T(2,128)(2,1)}), bf16[8,2,8192]{2,1,0:T(2,128)(2,1)}, u32[]{:S(2)}, u32[]{:S(2)}) async-start(bf16[8,2,8192]{2,1,0:T(2,128)(2,1)} %reshape.317), calls=%async_computation.1 | async-start | bytes 524288 | tf_op jit(solution)/shard_map/all_to_all | solution.py:172
  50.1 1.6 copy.134
  51.8 1.2 reshape.316
  53.0 0.7 copy-done.6
  53.9 0.9 reshape.296
  54.8 4.5 %all-to-all-done.1 = bf16[8,2,8192]{2,1,0:T(2,128)(2,1)} async-done(((bf16[8,2,8192]{2,1,0:T(2,128)(2,1)}), bf16[8,2,8192]{2,1,0:T(2,128)(2,1)}, u32[]{:S(2)}, u32[]{:S(2)}) %all-to-all-start.1) | async-done | bytes 262176 | tf_op jit(solution)/shard_map/all_to_all | solution.py:172
  59.4 1.2 reshape.318
  60.6 0.7 copy-done.1
  61.4 1.8 fusion.75
  63.1 0.4 multiply_reduce_fusion.3
  63.6 0.6 copy-done.17
  64.2 1.2 fusion.44
  65.8 0.7 copy-done.12
  66.6 1.2 fusion.1
  67.8 3.3 %multiply_reduce_fusion.1 = (f32[32,4,8]{2,1,0:T(4,128)}, f32[32,4,8,8]{2,3,1,0:T(8,128)}) fusion(f32[32,4,8,8]{2,3,1,0:T(8,128)} %fusion.44, bf16[8,32,4,64]{3,1,2,0:T(8,128)(2,1)} %copy-done.12, bf16[8,32,4,64]{3,1,2,0:T(8,128)(2,1)} %copy-done.14), kind=kOutput, calls=%fused_computation.46 | convolution fusion | flops 1081351 | bytes 331776 | tf_op jit(solution)/shard_map/div | solution.py:49
  71.1 1.4 multiply_convert_fusion.1
  72.4 2.0 fusion.49
  74.5 1.1 fusion.41
  75.6 2.4 fusion.46
  78.0 1.1 copy.185
  79.2 2.1 fusion.11
  81.4 1.0 fusion.22
  82.6 1.3 copy.109
  83.9 1.9 reshape.297
  85.9 1.1 convolution_convert_fusion.2
  87.0 17.4 %all-reduce.6.cloned.1.call-done = bf16[8,32,512]{2,1,0:T(8,128)(2,1)} async-done(((bf16[8,32,512]{2,1,0:T(8,128)(2,1)}), bf16[8,32,512]{2,1,0:T(8,128)(2,1)}) %all-reduce.6.cloned.1.call-update) | async-done | bytes 262160 | tf_op jit(solution)/shard_map/psum | solution.py:155
  104.4 1.7 fusion.7
  106.1 5.9 %all-to-all-start.2 = ((bf16[8,32,512]{2,1,0:T(8,128)(2,1)}), bf16[8,32,512]{2,1,0:T(8,128)(2,1)}, u32[]{:S(2)}, u32[]{:S(2)}) async-start(bf16[8,32,512]{2,1,0:T(8,128)(2,1)} %fusion.7), calls=%async_computation.2 | async-start | bytes 524288 | tf_op jit(solution)/shard_map/all_to_all | solution.py:181
  112.0 2.4 fusion.3
  114.4 1.1 copy.113
  115.5 1.1 copy.117
  116.8 0.9 copy.114
  117.7 1.1 convolution_bitcast_fusion.1
  118.8 1.5 fusion.28
  120.3 1.2 all-to-all-done.2
  121.5 1.4 convolution_convert_fusion.5
  123.7 0.7 copy-done.23
  125.2 0.5 copy-done.11
  126.3 1.1 convolution_convert_fusion.1
  127.4 2.0 convolution_bitcast_fusion.2
  129.5 1.7 copy.119
  131.1 4.1 %pad_maximum_fusion = f32[512,8,256]{2,0,1:T(8,128)} fusion(f32[512,1,256]{2,0,1:T(8,128)} %convolution_bitcast_fusion.1, f32[512,3,256]{2,0,1:T(8,128)S(1)} %fusion.28, f32[512,1,256]{2,0,1:T(8,128)} %convolution_bitcast_fusion.2, f32[512,3,256]{2,0,1:T(8,128)} %copy.119), kind=kLoop, calls=%fused_computation | loop fusion | flops 3145728 | bytes 8388608 | tf_op jit(solution)/shard_map/concatenate | solution.py:187
  135.2 10.7 %all-reduce.8.cloned.1.call-done = bf16[256,512]{1,0:T(8,128)(2,1)} async-done(((bf16[256,512]{1,0:T(8,128)(2,1)}), bf16[256,512]{1,0:T(8,128)(2,1)}) %all-reduce.8.cloned.1.call-update) | async-done | bytes 262160 | tf_op jit(solution)/shard_map/psum | solution.py:155
  145.9 1.8 fusion.20
  147.7 91.2 %reduce-scatter.2.cloned.1.call-done = f32[64,8,256]{2,0,1:T(8,128)} async-done(((f32[512,8,256]{2,0,1:T(8,128)}), f32[64,8,256]{2,0,1:T(8,128)}) %reduce-scatter.2.cloned.1.call-update) | async-done | bytes 524304 | tf_op jit(solution)/shard_map/reduce_scatter | solution.py:186
  239.0 1.1 broadcast_multiply_fusion
  240.1 1.1 copy.120
  (87 shorter events, 4.6 us)
Async XLA Ops:
  7.2 30.8 %all-reduce.4.cloned.1.call-start = ((), (), s32[]{:S(2)}) async-start(), calls=%async_computation.4 | async-start | bytes 524288 | tf_op jit(solution)/shard_map/psum | solution.py:155
  7.2 4.4 %copy-start.3 = (bf16[512,8,256]{2,1,0:T(8,128)(2,1)S(1)}, bf16[512,8,256]{2,1,0:T(8,128)(2,1)}, u32[]{:S(2)}) copy-start(bf16[512,8,256]{2,1,0:T(8,128)(2,1)} %param.4) | copy-start | bytes 6291460
  12.3 1.0 copy-start.10
  13.2 0.9 copy-start.8
  13.8 0.6 copy-start.26
  13.8 0.6 copy-start.28
  14.1 0.7 copy-start.20
  14.1 0.7 copy-start.22
  14.8 1.0 copy-start.15
  23.5 20.6 %all-to-all-start = ((bf16[8,2,8192]{2,1,0:T(2,128)(2,1)}), bf16[8,2,8192]{2,1,0:T(2,128)(2,1)}, u32[]{:S(2)}, u32[]{:S(2)}) async-start(bf16[8,2,8192]{2,1,0:T(2,128)(2,1)} %reshape.315), calls=%async_computation | async-start | bytes 524288 | tf_op jit(solution)/shard_map/all_to_all | solution.py:173
  44.1 15.3 %all-to-all-start.1 = ((bf16[8,2,8192]{2,1,0:T(2,128)(2,1)}), bf16[8,2,8192]{2,1,0:T(2,128)(2,1)}, u32[]{:S(2)}, u32[]{:S(2)}) async-start(bf16[8,2,8192]{2,1,0:T(2,128)(2,1)} %reshape.317), calls=%async_computation.1 | async-start | bytes 524288 | tf_op jit(solution)/shard_map/all_to_all | solution.py:172
  49.9 54.5 %all-reduce.6.cloned.1.call-start = ((), (), s32[]{:S(2)}) async-start(), calls=%async_computation.5 | async-start | bytes 524288 | tf_op jit(solution)/shard_map/psum | solution.py:155
  50.1 3.6 %copy-start.16 = (bf16[512,1,256]{2,1,0:T(2,128)(2,1)S(1)}, bf16[512,1,256]{2,1,0:T(2,128)(2,1)}, u32[]{:S(2)}) copy-start(bf16[512,1,256]{2,1,0:T(2,128)(2,1)} %get-tuple-element.21) | copy-start | bytes 786436
  53.0 0.7 copy-start.6
  60.6 0.8 copy-start.1
  61.4 2.9 %copy-start.19 = (bf16[8,32,4,64]{3,2,1,0:T(4,128)(2,1)S(1)}, bf16[8,32,4,64]{3,2,1,0:T(4,128)(2,1)}, u32[]{:S(2)}) copy-start(bf16[8,32,4,64]{3,2,1,0:T(4,128)(2,1)} %reshape.296) | copy-start | bytes 393220
  63.5 0.7 copy-start.17
  64.2 1.2 copy-start.24
  65.8 0.7 copy-start.12
  65.8 0.8 copy-start.14
  71.1 3.4 %copy-start.13 = (bf16[8,32,4,64]{3,1,2,0:T(8,128)(2,1)S(1)}, bf16[8,32,4,64]{3,1,2,0:T(8,128)(2,1)}, u32[]{:S(2)}) copy-start(bf16[8,32,4,64]{3,1,2,0:T(8,128)(2,1)} %copy-done.12) | copy-start | bytes 393220
  78.0 3.3 %copy-start.4 = (f32[32,4,64,8]{2,3,1,0:T(8,128)S(1)}, f32[32,4,64,8]{2,3,1,0:T(8,128)}, u32[]{:S(2)}) copy-start(f32[32,4,64,8]{2,3,1,0:T(8,128)} %fusion.49) | copy-start | bytes 786436
  78.0 3.3 %copy-start.5 = (f32[32,4,64,8]{2,3,1,0:T(8,128)S(1)}, f32[32,4,64,8]{2,3,1,0:T(8,128)}, u32[]{:S(2)}) copy-start(f32[32,4,64,8]{2,3,1,0:T(8,128)} %fusion.41) | copy-start | bytes 786436
  78.0 3.3 %copy-start.25 = (f32[8,32,4]{1,2,0:T(4,128)S(1)}, f32[8,32,4]{1,2,0:T(4,128)}, u32[]{:S(2)}) copy-start(f32[8,32,4]{1,2,0:T(4,128)} %copy-done.24) | copy-start | bytes 12292
  82.6 3.3 %copy-start = (bf16[512,3,256]{0,2,1:T(8,128)(2,1)S(1)}, bf16[512,3,256]{0,2,1:T(8,128)(2,1)}, u32[]{:S(2)}) copy-start(bf16[512,3,256]{0,2,1:T(8,128)(2,1)} %copy.134) | copy-start | bytes 2359300
  83.9 20.5 %copy-start.7 = (bf16[1,256,512]{2,1,0:T(8,128)(2,1)S(1)}, bf16[1,256,512]{2,1,0:T(8,128)(2,1)}, u32[]{:S(2)}) copy-start(bf16[1,256,512]{2,1,0:T(8,128)(2,1)} %copy-done.6) | copy-start | bytes 786436
  86.9 25.1 %copy-start.18 = (bf16[8,32,4,64]{3,1,2,0:T(8,128)(2,1)S(1)}, bf16[8,32,4,64]{3,1,2,0:T(8,128)(2,1)}, u32[]{:S(2)}) copy-start(bf16[8,32,4,64]{3,1,2,0:T(8,128)(2,1)} %copy-done.17) | copy-start | bytes 393220
  106.1 8.3 %copy-start.2 = (bf16[256,1,512]{2,1,0:T(2,128)(2,1)S(1)}, bf16[256,1,512]{2,1,0:T(2,128)(2,1)}, u32[]{:S(2)}) copy-start(bf16[256,1,512]{2,1,0:T(2,128)(2,1)} %copy-done.1) | copy-start | bytes 786436
  106.1 15.4 %all-to-all-start.2 = ((bf16[8,32,512]{2,1,0:T(8,128)(2,1)}), bf16[8,32,512]{2,1,0:T(8,128)(2,1)}, u32[]{:S(2)}, u32[]{:S(2)}) async-start(bf16[8,32,512]{2,1,0:T(8,128)(2,1)} %fusion.7), calls=%async_computation.2 | async-start | bytes 524288 | tf_op jit(solution)/shard_map/all_to_all | solution.py:181
  112.0 34.0 %all-reduce.8.cloned.1.call-start = ((), (), s32[]{:S(2)}) async-start(), calls=%async_computation.6 | async-start | bytes 524288 | tf_op jit(solution)/shard_map/psum | solution.py:155
  123.5 0.9 copy-start.23
  123.5 1.2 copy-start.21
  123.5 1.2 copy-start.27
  123.6 1.2 copy-start.29
  124.7 1.0 copy-start.11
  125.1 1.2 copy-start.9
  127.4 111.6 %reduce-scatter.2.cloned.1.call-start = ((), (), s32[]{:S(2)}) async-start(), calls=%async_computation.7 | async-start | bytes 4718592 | tf_op jit(solution)/shard_map/reduce_scatter | solution.py:186
Sparse Core Ops, SparseCore 0:
  17.0 20.9 all-reduce.3
  87.1 17.2 all-reduce.5
  127.5 18.3 all-reduce.7
  149.9 89.0 reduce-scatter.1
where the time goes:
time: 249 us; the launch traced here: 248 us
  waiting for transfers between devices  132 us (53%)
  local copies, waits for them, and re-layouts  33 us (13%)
  matrix products  27.3 us (11%)
  other arithmetic  21.5 us (9%)
  starting transfers between devices  19.3 us (8%)
  between operations  14.3 us (6%)
    reduce_scatter x1, waiting for transfers between devices, on_device(): lax.psum_scatter(jnp.concatenate((weight_terms(flat_row, stacked_row, gra...  91.2 us
    psum x3, waiting for transfers between devices, head_sum(): lax.psum(partial_value.astype(jnp.bfloat16), 'head').astype(jnp.float32)  35.4 us
    unnamed x70, local copies, waits for them, and re-layouts  17.2 us
    all_to_all x1, starting transfers between devices, on_device(): lax.all_to_all(cotangent, 'row', split_axis=1, concat_axis=0, tiled=True)  7.26 us
    all_to_all x1, starting transfers between devices, on_device(): lax.all_to_all(grad_mid, 'row', split_axis=0, concat_axis=1, tiled=True)  5.9 us
    unnamed x2, other arithmetic  5.87 us
    all_to_all x1, starting transfers between devices, on_device(): lax.all_to_all(first_out, 'row', split_axis=1, concat_axis=0, tiled=True)  5.77 us
  transfers between devices with their start and end apart: 7, of which 6 were waited for; matrix products, arithmetic and copies ran while one was open for 14% of the time, Pallas kernels for 0%

commit v1 on v0

--- a/solution.py
+++ b/solution.py
@@ -1,8 +1,11 @@
+import functools
 import math
 
 import jax
 import jax.numpy as jnp
 from jax import lax
+from jax.experimental import pallas as pl
+from jax.experimental.pallas import tpu as pltpu
 from jax.sharding import PartitionSpec as P
 
 HEAD_DIM = 64
@@ -203,9 +206,339 @@
     return (latent_grad, weight_grad)
 
 
+MESH = pl.DeviceIdType.MESH
+F32, BF16 = jnp.float32, jnp.bfloat16
+
+
+def mm(left, right):
+    return jnp.dot(left, right, preferred_element_type=F32)
+
+
+def mm_t(left, right):
+    return lax.dot_general(left, right, (((1,), (1,)), ((), ())), preferred_element_type=F32)
+
+
+def t_mm(left, right):
+    return lax.dot_general(left, right, (((0,), (0,)), ((), ())), preferred_element_type=F32)
+
+
+def fused(
+    n, scale, x_ref, w_ref, ct_ref, lat_ref, wg_ref,
+    gcol, ycol, gmid, ysend, dsend, hsend, hrecv, fsend, frecv,
+    norm_s, inv_s, qkv_s, probs_s, att_s, grads_s, dstack, pstack,
+    xs, xr, zs, zr,
+    a_send, a_recv, h_send, h_recv, x_send, x_recv, z_send, z_recv,
+):
+    me, core = lax.axis_index("row"), lax.axis_index("head")
+    other = 1 - core
+    count, width = x_ref.shape
+    local = w_ref.shape[2]
+    block, half = count // n, width // 2
+    heads = local // HEAD_DIM
+    logit_scale = 2.0 / math.sqrt(HEAD_DIM)
+    pairs = n // 2
+    my_x, my_z = lax.rem(me, 2), me // 2
+    rows_here = width // n
+
+    peers = [(me, other)]
+    for step in range(1, n):
+        for which in (core, other):
+            peers.append((lax.rem(me + step, n), which))
+
+    def rows_of(position):
+        return pl.ds(pl.multiple_of(position * block, block), block)
+
+    def half_of(which):
+        return pl.ds(pl.multiple_of(which * half, half), half)
+
+    def exchange_copy(phase, index, src, dst, source, target):
+        row, which = source
+        return pltpu.make_async_remote_copy(
+            src_ref=src,
+            dst_ref=dst.at[which, rows_of(row), :],
+            send_sem=a_send.at[phase, index],
+            recv_sem=a_recv.at[phase, which * n + row],
+            device_id={"row": target[0], "head": target[1]},
+            device_id_type=MESH,
+        )
+
+    def exchange_start(phase, view, dst):
+        copies = []
+        for index, target in enumerate(peers):
+            copy = exchange_copy(phase, index, view(target[0]), dst, (me, core), target)
+            copy.start()
+            copies.append(copy)
+        return copies
+
+    def exchange_wait(phase, view, dst):
+        for index, source in enumerate(peers):
+            exchange_copy(phase, index, view(me), dst, source, source).wait_recv()
+
+    def head_copy(phase, src, dst):
+        return pltpu.make_async_remote_copy(
+            src_ref=src, dst_ref=dst, send_sem=h_send.at[phase], recv_sem=h_recv.at[phase],
+            device_id={"row": me, "head": other}, device_id_type=MESH,
+        )
+
+    def x_copy(layer, slot):
+        return pltpu.make_async_remote_copy(
+            src_ref=xs.at[layer, slot, 1 - my_x], dst_ref=xr.at[layer, slot],
+            send_sem=x_send.at[layer, slot], recv_sem=x_recv.at[layer, slot],
+            device_id={"row": me + 1 - 2 * my_x, "head": core}, device_id_type=MESH,
+        )
+
+    def z_copy(layer, slot, index, source_z, target_z):
+        return pltpu.make_async_remote_copy(
+            src_ref=zs.at[layer, slot, target_z], dst_ref=zr.at[layer, slot, source_z],
+            send_sem=z_send.at[layer, slot, index], recv_sem=z_recv.at[layer, slot, source_z],
+            device_id={"row": 2 * target_z + my_x, "head": core}, device_id_type=MESH,
+        )
+
+    def scatter_first(layer, slot, product):
+        rounded = product.astype(BF16)
+        for target in range(n):
+            xs[layer, slot, target % 2, target // 2] = rounded[
+                target * rows_here : (target + 1) * rows_here
+            ]
+        x_copy(layer, slot).start()
+
+    def scatter_second(layer, slot):
+        x_copy(layer, slot).wait_recv()
+        total = xs[layer, slot, my_x].astype(F32) + xr[layer, slot].astype(F32)
+        zs[layer, slot] = total.astype(BF16)
+        for step in range(1, pairs):
+            z_copy(layer, slot, step, my_z, lax.rem(my_z + step, pairs)).start()
+
+    def scatter_last(layer, slot):
+        total = zs[layer, slot, my_z].astype(F32)
+        for step in range(1, pairs):
+            source = lax.rem(my_z + step, pairs)
+            z_copy(layer, slot, step, source, source).wait_recv()
+            total = total + zr[layer, slot, source].astype(F32)
+        wg_ref[:, 4 * layer + slot, :] = total * scale
+
+    lane = lax.broadcasted_iota(jnp.int32, (1, local), 1) // HEAD_DIM
+    head_mask = [jnp.where(lane == head, 1.0, 0.0).astype(BF16) for head in range(heads)]
+    spread = jnp.where(
+        lax.broadcasted_iota(jnp.int32, (local, local), 0) // HEAD_DIM
+        == lax.broadcasted_iota(jnp.int32, (local, local), 1) // HEAD_DIM,
+        1.0 / HEAD_DIM, 0.0,
+    ).astype(BF16)
+    spread_twice = jnp.concatenate([spread, spread], 0)
+
+    def head_mean(values):
+        high = values.astype(BF16)
+        low = (values - high.astype(F32)).astype(BF16)
+        return mm(jnp.concatenate([high, low], 1), spread_twice)
+
+    def masked(values):
+        return jnp.concatenate([values * mask for mask in head_mask], 0)
+
+    def forward(layer, z):
+        query, key, value = (mm(z, w_ref[4 * layer + i]) for i in range(3))
+        both = jnp.concatenate([query, key], 0)
+        inverse = lax.rsqrt(head_mean(both * both) + epsilon)
+        normed = both * inverse
+        norm_s[layer] = normed
+        inv_s[layer] = inverse
+        qkv_s[layer, 0] = normed[:count].astype(BF16)
+        qkv_s[layer, 1] = normed[count:].astype(BF16)
+        qkv_s[layer, 2] = value.astype(BF16)
+        query_b, key_b = qkv_s[layer, 0], qkv_s[layer, 1]
+        keep = None
+        if layer == 1:
+            keep = jnp.where(
+                lax.rem(lax.broadcasted_iota(jnp.int32, (count, count), 0), block)
+                == lax.rem(lax.broadcasted_iota(jnp.int32, (count, count), 1), block),
+                1.0, 0.0,
+            )
+        for head in range(heads):
+            expo = jnp.exp(logit_scale * mm_t(query_b * head_mask[head], key_b))
+            if keep is not None:
+                expo = expo * keep
+            probs = expo * (1.0 / jnp.sum(expo, axis=-1, keepdims=True))
+            probs_s[layer, head] = probs
+            pstack[layer, head * count : (head + 1) * count, :] = probs.astype(BF16)
+        wide = jnp.concatenate(
+            [pstack[layer, head * count : (head + 1) * count, :] for head in range(heads)], 1
+        )
+        att_s[layer] = mm(wide, masked(qkv_s[layer, 2])).astype(BF16)
+
+    def backward(layer, grad, after_value):
+        query_b, key_b, value_b = qkv_s[layer, 0], qkv_s[layer, 1], qkv_s[layer, 2]
+        grad_att = mm(grad, w_ref[4 * layer + 3]).astype(BF16)
+        grads_s[layer, 2] = t_mm(pstack[layer], masked(grad_att)).astype(BF16)
+        after_value()
+        for head in range(heads):
+            grad_probs = mm_t(grad_att * head_mask[head], value_b)
+            probs = probs_s[layer, head]
+            delta = jnp.sum(probs * grad_probs, axis=-1, keepdims=True)
+            dstack[head * count : (head + 1) * count, :] = (
+                probs * (grad_probs - delta)
+            ).astype(BF16)
+        wide = jnp.concatenate(
+            [dstack[head * count : (head + 1) * count, :] for head in range(heads)], 1
+        )
+        grad_query = mm(wide, masked(key_b))
+        grad_key = t_mm(dstack[...], masked(query_b))
+        grads = logit_scale * jnp.concatenate([grad_query, grad_key], 0)
+        normed = norm_s[layer]
+        out = (inv_s[layer] * (grads - normed * head_mean(grads * normed))).astype(BF16)
+        grads_s[layer, 0] = out[:count]
+        grads_s[layer, 1] = out[count:]
+
+    def input_grad(layer, which):
+        total = mm_t(grads_s[layer, 0], w_ref[4 * layer, half_of(which), :])
+        for i in (1, 2):
+            total = total + mm_t(grads_s[layer, i], w_ref[4 * layer + i, half_of(which), :])
+        return total
+
+    def joined(ref):
+        return jnp.concatenate([ref[0], ref[1]], 1)
+
+    barrier = pltpu.get_barrier_semaphore()
+    for row, which in peers:
+        pl.semaphore_signal(
+            barrier, inc=1, device_id={"row": row, "head": which}, device_id_type=MESH
+        )
+    pl.semaphore_wait(barrier, len(peers))
+
+    def ct_view(row):
+        return ct_ref.at[rows_of(row), half_of(core)]
+
+    def y_view(row):
+        return ysend.at[rows_of(row), :]
+
+    def d_view(row):
+        return dsend.at[rows_of(row), :]
+
+    copies = exchange_start(0, ct_view, gcol)
+    gcol[core, rows_of(me), :] = ct_ref[rows_of(me), half_of(core)]
+
+    forward(0, x_ref[...])
+    hsend[0] = mm_t(att_s[0], w_ref[3, half_of(other), :]).astype(BF16)
+    first_half = head_copy(0, hsend.at[0], hrecv.at[0])
+    first_half.start()
+    mixed = mm_t(att_s[0], w_ref[3, half_of(core), :]) + x_ref[:, half_of(core)].astype(F32)
+    first_half.wait_recv()
+    ysend[...] = (mixed + hrecv[0].astype(F32)).astype(BF16)
+    copies += exchange_start(1, y_view, ycol)
+    ycol[core, rows_of(me), :] = ysend[rows_of(me), :]
+
+    exchange_wait(0, ct_view, gcol)
+    exchange_wait(1, y_view, ycol)
+    columns = joined(ycol)
+    forward(1, columns)
+    backward(1, joined(gcol), lambda: None)
+    hsend[1] = input_grad(1, other).astype(BF16)
+    second_half = head_copy(1, hsend.at[1], hrecv.at[1])
+    second_half.start()
+    mixed = input_grad(1, core) + gcol[core].astype(F32)
+    second_half.wait_recv()
+    dsend[...] = (mixed + hrecv[1].astype(F32)).astype(BF16)
+    copies += exchange_start(2, d_view, gmid)
+    gmid[core, rows_of(me), :] = dsend[rows_of(me), :]
+    turned = joined(ycol).T
+    for slot in range(3):
+        scatter_first(1, slot, mm(turned, grads_s[1, slot]))
+    scatter_first(1, 3, mm(joined(gcol).T, att_s[1]))
+
+    exchange_wait(2, d_view, gmid)
+    grad_first = joined(gmid)
+    scatter_first(0, 3, mm(grad_first.T, att_s[0]))
+
+    def after_value():
+        scatter_first(0, 2, mm(x_ref[...].T, grads_s[0, 2]))
+        for slot in range(4):
+            scatter_second(1, slot)
+
+    backward(0, grad_first, after_value)
+    turned = x_ref[...].T
+    scatter_first(0, 0, mm(turned, grads_s[0, 0]))
+    scatter_first(0, 1, mm(turned, grads_s[0, 1]))
+    for which in range(2):
+        fsend[which] = input_grad(0, which).astype(BF16)
+    full = head_copy(2, fsend, frecv)
+    full.start()
+    scatter_second(0, 3)
+    scatter_second(0, 2)
+    full.wait_recv()
+    for which in range(2):
+        lat_ref[:, which * half : (which + 1) * half] = (
+            gmid[which].astype(F32) + (fsend[which].astype(F32) + frecv[which].astype(F32))
+        ).astype(BF16)
+    for slot in range(4):
+        scatter_last(1, slot)
+    scatter_second(0, 0)
+    scatter_second(0, 1)
+    for slot in (3, 2, 0, 1):
+        scatter_last(0, slot)
+
+    for copy in copies:
+        copy.wait_send()
+    for copy in (first_half, second_half, full):
+        copy.wait_send()
+    for layer in range(2):
+        for slot in range(4):
+            x_copy(layer, slot).wait_send()
+            for step in range(1, pairs):
+                z_copy(layer, slot, step, my_z, lax.rem(my_z + step, pairs)).wait_send()
+
+
+def fused_call(latent, weights, cotangent):
+    n = lax.axis_size("row")
+    _, count, width = latent.shape
+    local = weights.shape[2]
+    heads, block, half, rows_here = local // HEAD_DIM, count // n, width // 2, width // n
+    scale = 1.0 / math.sqrt(n * count)
+    vmem = pl.BlockSpec(memory_space=pltpu.VMEM)
+    dma = pltpu.SemaphoreType.DMA
+    halves = pltpu.VMEM((2, count, half), BF16)
+    latent_grad, weight_grad = pl.pallas_call(
+        functools.partial(fused, n, scale),
+        out_shape=(
+            jax.ShapeDtypeStruct((count, width), BF16),
+            jax.ShapeDtypeStruct((rows_here, 8, local), F32),
+        ),
+        in_specs=[vmem] * 3,
+        out_specs=(vmem, vmem),
+        scratch_shapes=[
+            halves, halves, halves,
+            pltpu.VMEM((count, half), BF16), pltpu.VMEM((count, half), BF16),
+            halves, halves, halves, halves,
+            pltpu.VMEM((2, 2 * count, local), F32), pltpu.VMEM((2, 2 * count, local), F32),
+            pltpu.VMEM((2, 3, count, local), BF16),
+            pltpu.VMEM((2, heads, count, count), F32),
+            pltpu.VMEM((2, count, local), BF16),
+            pltpu.VMEM((2, 3, count, local), BF16),
+            pltpu.VMEM((heads * count, count), BF16),
+            pltpu.VMEM((2, heads * count, count), BF16),
+            pltpu.VMEM((2, 4, 2, n // 2, rows_here, local), BF16),
+            pltpu.VMEM((2, 4, n // 2, rows_here, local), BF16),
+            pltpu.VMEM((2, 4, n // 2, rows_here, local), BF16),
+            pltpu.VMEM((2, 4, n // 2, rows_here, local), BF16),
+            dma((3, 2 * n)), dma((3, 2 * n)), dma((3,)), dma((3,)),
+            dma((2, 4)), dma((2, 4)), dma((2, 4, n // 2)), dma((2, 4, n // 2)),
+        ],
+        compiler_params=pltpu.CompilerParams(
+            collective_id=0, has_side_effects=True, vmem_limit_bytes=44 * 1024 * 1024
+        ),
+    )(latent[0], jnp.transpose(weights, (1, 0, 2)), cotangent[0])
+    return (latent_grad[None], weight_grad)
+
+
+def either(latent, weights, cotangent):
+    n = lax.axis_size("row")
+    rows, cols, width = latent.shape
+    aligned = n % 2 == 0 and cols % (16 * n) == 0 and width % (16 * n) == 0
+    if rows == 1 and aligned and lax.axis_size("head") == 2:
+        return fused_call(latent, weights, cotangent)
+    return on_device(latent, weights, cotangent)
+
+
 def solution(mesh):
     in_specs = (P(("grp", "row"), None, None), P(None, None, "head"), P(("grp", "row"), None, None))
     out_specs = (P(("grp", "row"), None, None), P(("grp", "row"), None, "head"))
     return jax.shard_map(
-        on_device, mesh=mesh, in_specs=in_specs, out_specs=out_specs, check_vma=False
-    )
+        either, mesh=mesh, in_specs=in_specs, out_specs=out_specs, check_vma=False
+    )

time: 249 us -> 61.4 us (0.25)
  waiting for transfers between devices: 132 us -> 0 us
  Pallas kernels: 0 us -> 57 us
  local copies, waits for them, and re-layouts: 33 us -> 3.58 us
  matrix products: 27.3 us -> 0 us
  other arithmetic: 21.5 us -> 0 us
  starting transfers between devices: 19.3 us -> 0 us
  between operations: 14.3 us -> 0.68 us
    reduce_scatter x1 -> x0, waiting for transfers between devices: 91.2 us -> none  [on_device(): lax.psum_scatter(jnp.concatenate((weight_terms(flat_row, stacked_row, gra...]
    pallas_call x0 -> x1, Pallas kernels: none -> 57 us  [fused_call(): pl.pallas_call(functools.partial(fused, n, scale), out_shape=(jax.ShapeDt...]
    psum x3 -> x0, waiting for transfers between devices: 35.4 us -> none  [head_sum(): lax.psum(partial_value.astype(jnp.bfloat16), 'head').astype(jnp.float32)]
    dot_general x22 -> x0, matrix products: 23.6 us -> none  [the longest x2 3.09 us: weight_terms(): lax.dot_general(grad_flat, attention_output, contract, preferred_element_...]
    all_to_all x3 -> x0, starting transfers between devices: 18.9 us -> none  [the longest x1 7.26 us: on_device(): lax.all_to_all(cotangent, 'row', split_axis=1, concat_axis=0, tiled=True)]
    unnamed x70 -> x7, local copies, waits for them, and re-layouts: 17.2 us -> 3.58 us
    convert_element_type x7 -> x0, other arithmetic: 6.44 us -> none  [the longest x1 1.8 us: on_device(): latent_grad = (grad_first.astype(jnp.float32) + head_sum(partial_row).res...]
    unnamed x2 -> x0, other arithmetic: 5.87 us -> none
  transfers between devices with their start and end apart: 7 -> 0, of which waited for: 6 -> 0; matrix products, arithmetic and copies ran while one was open for 14% -> 0% of each run, Pallas kernels for 0% -> 0%
where the time goes in v1:
time: 61.4 us; the launch traced here: 61.3 us
  Pallas kernels  57 us (93%)
  local copies, waits for them, and re-layouts  3.58 us (6%)
  between operations  0.68 us (1%)
    pallas_call x1, Pallas kernels, fused_call(): pl.pallas_call(functools.partial(fused, n, scale), out_shape=(jax.ShapeDt...  57 us
    unnamed x7, local copies, waits for them, and re-layouts  3.58 us

profile of v1, /device:TPU:0, one launch (start us, length us, event | category | flops | bytes accessed | tf_op | source)
XLA Modules:
  0.0 61.3 jit_solution(4087781588623087695)
XLA Ops:
  0.6 0.0 copy-start
  0.6 0.0 copy-start.1
  0.6 2.1 %copy.7 = bf16[512,8,256]{2,0,1:T(8,128)(2,1)S(1)} copy(bf16[512,8,256]{2,1,0:T(8,128)(2,1)} %param.4) | data formatting | bytes 4194304 | tf_op args[1]
  2.7 0.0 copy-done
  2.7 0.0 copy-done.1
  2.7 57.0 %shard_map.50 = (bf16[256,512]{1,0:T(8,128)(2,1)S(1)}, f32[64,8,256]{2,1,0:T(8,128)S(1)}) custom-call(bf16[256,512]{1,0:T(8,128)(2,1)S(1)} %bitcast.7, bf16[8,512,256]{2,1,0:T(8,128)(2,1)S(1)} %bitcast.6, bf16[256,512]{1,0:T(8,128)(2,1)S(1)} %bitcast.8), custom_call_target="tpu_custom_call" | custom-call | tf_op jit(solution)/shard_map/pallas_call | solution.py:497
  59.8 0.7 %copy.10 = bf16[1,256,512]{2,1,0:T(8,128)(2,1)} copy(bf16[1,256,512]{2,1,0:T(8,128)(2,1)S(1)} %bitcast.9) | data formatting | bytes 524288
  60.5 0.8 %copy.11 = f32[64,8,256]{2,1,0:T(8,128)} copy(f32[64,8,256]{2,1,0:T(8,128)S(1)} %get-tuple-element.9) | data formatting | bytes 1048576
Async XLA Ops:
  0.6 2.1 %copy-start = (bf16[1,256,512]{2,1,0:T(8,128)(2,1)S(1)}, bf16[1,256,512]{2,1,0:T(8,128)(2,1)}, u32[]{:S(2)}) copy-start(bf16[1,256,512]{2,1,0:T(8,128)(2,1)} %param.3) | copy-start | bytes 786436
  0.6 2.1 %copy-start.1 = (bf16[1,256,512]{2,1,0:T(8,128)(2,1)S(1)}, bf16[1,256,512]{2,1,0:T(8,128)(2,1)}, u32[]{:S(2)}) copy-start(bf16[1,256,512]{2,1,0:T(8,128)(2,1)} %param.5) | copy-start | bytes 786436

commit v2 on v1

--- a/solution.py
+++ b/solution.py
@@ -251,7 +251,7 @@
     def half_of(which):
         return pl.ds(pl.multiple_of(which * half, half), half)
 
-    def exchange_copy(phase, index, src, dst, source, target):
+    def block_copy(phase, index, src, dst, source, target):
         row, which = source
         return pltpu.make_async_remote_copy(
             src_ref=src,
@@ -263,16 +263,26 @@
         )
 
     def exchange_start(phase, view, dst):
-        copies = []
-        for index, target in enumerate(peers):
-            copy = exchange_copy(phase, index, view(target[0]), dst, (me, core), target)
-            copy.start()
-            copies.append(copy)
-        return copies
+        for step in range(1, n):
+            row = lax.rem(me + step, n)
+            block_copy(phase, step, view(row), dst, (me, core), (row, core)).start()
+        block_copy(phase, n, view(me), dst, (me, core), (me, other)).start()
+
+    def exchange_pass(phase, view, dst):
+        for step in range(1, n):
+            row = lax.rem(me + n - step, n)
+            block_copy(phase, step, view(me), dst, (row, core), (row, core)).wait_recv()
+            here = dst.at[core, rows_of(row), :]
+            block_copy(phase, n + step, here, dst, (row, core), (me, other)).start()
 
     def exchange_wait(phase, view, dst):
-        for index, source in enumerate(peers):
-            exchange_copy(phase, index, view(me), dst, source, source).wait_recv()
+        for step in range(n):
+            row = lax.rem(me + n - step, n)
+            block_copy(phase, step, view(me), dst, (row, other), (me, other)).wait_recv()
+
+    def exchange_end(phase, view, dst):
+        for index in range(1, 2 * n):
+            block_copy(phase, index, view(me), dst, (me, core), (me, other)).wait_send()
 
     def head_copy(phase, src, dst):
         return pltpu.make_async_remote_copy(
@@ -412,7 +422,7 @@
     def d_view(row):
         return dsend.at[rows_of(row), :]
 
-    copies = exchange_start(0, ct_view, gcol)
+    exchange_start(0, ct_view, gcol)
     gcol[core, rows_of(me), :] = ct_ref[rows_of(me), half_of(core)]
 
     forward(0, x_ref[...])
@@ -422,44 +432,46 @@
     mixed = mm_t(att_s[0], w_ref[3, half_of(core), :]) + x_ref[:, half_of(core)].astype(F32)
     first_half.wait_recv()
     ysend[...] = (mixed + hrecv[0].astype(F32)).astype(BF16)
-    copies += exchange_start(1, y_view, ycol)
+    exchange_start(1, y_view, ycol)
     ycol[core, rows_of(me), :] = ysend[rows_of(me), :]
 
+    exchange_pass(0, ct_view, gcol)
+    exchange_pass(1, y_view, ycol)
     exchange_wait(0, ct_view, gcol)
     exchange_wait(1, y_view, ycol)
     columns = joined(ycol)
     forward(1, columns)
-    backward(1, joined(gcol), lambda: None)
+    scatter_first(1, 3, mm(joined(gcol).T, att_s[1]))
+    turned = columns.T
+    backward(1, joined(gcol), lambda: scatter_first(1, 2, mm(turned, grads_s[1, 2])))
     hsend[1] = input_grad(1, other).astype(BF16)
     second_half = head_copy(1, hsend.at[1], hrecv.at[1])
     second_half.start()
     mixed = input_grad(1, core) + gcol[core].astype(F32)
     second_half.wait_recv()
     dsend[...] = (mixed + hrecv[1].astype(F32)).astype(BF16)
-    copies += exchange_start(2, d_view, gmid)
+    exchange_start(2, d_view, gmid)
     gmid[core, rows_of(me), :] = dsend[rows_of(me), :]
-    turned = joined(ycol).T
-    for slot in range(3):
+    for slot in range(2):
         scatter_first(1, slot, mm(turned, grads_s[1, slot]))
-    scatter_first(1, 3, mm(joined(gcol).T, att_s[1]))
-
+    for slot in (3, 2):
+        scatter_second(1, slot)
+
+    exchange_pass(2, d_view, gmid)
     exchange_wait(2, d_view, gmid)
     grad_first = joined(gmid)
     scatter_first(0, 3, mm(grad_first.T, att_s[0]))
 
-    def after_value():
-        scatter_first(0, 2, mm(x_ref[...].T, grads_s[0, 2]))
-        for slot in range(4):
-            scatter_second(1, slot)
-
-    backward(0, grad_first, after_value)
     turned = x_ref[...].T
+    backward(0, grad_first, lambda: scatter_first(0, 2, mm(turned, grads_s[0, 2])))
     scatter_first(0, 0, mm(turned, grads_s[0, 0]))
     scatter_first(0, 1, mm(turned, grads_s[0, 1]))
     for which in range(2):
         fsend[which] = input_grad(0, which).astype(BF16)
     full = head_copy(2, fsend, frecv)
     full.start()
+    scatter_second(1, 0)
+    scatter_second(1, 1)
     scatter_second(0, 3)
     scatter_second(0, 2)
     full.wait_recv()
@@ -474,8 +486,9 @@
     for slot in (3, 2, 0, 1):
         scatter_last(0, slot)
 
-    for copy in copies:
-        copy.wait_send()
+    exchange_end(0, ct_view, gcol)
+    exchange_end(1, y_view, ycol)
+    exchange_end(2, d_view, gmid)
     for copy in (first_half, second_half, full):
         copy.wait_send()
     for layer in range(2):

time: 61.4 us -> 53.7 us (0.87)
  Pallas kernels: 57 us -> 49.2 us
    pallas_call x1, Pallas kernels: 57 us -> 49.2 us  [fused_call(): pl.pallas_call(functools.partial(fused, n, scale), out_shape=(jax.ShapeDt...]
where the time goes in v2:
time: 53.7 us; the launch traced here: 53.5 us
  Pallas kernels  49.2 us (92%)
  local copies, waits for them, and re-layouts  3.58 us (7%)
  between operations  0.68 us (1%)
    pallas_call x1, Pallas kernels, fused_call(): pl.pallas_call(functools.partial(fused, n, scale), out_shape=(jax.ShapeDt...  49.2 us
    unnamed x7, local copies, waits for them, and re-layouts  3.58 us

profile of v2, /device:TPU:0, one launch (start us, length us, event | category | flops | bytes accessed | tf_op | source)
XLA Modules:
  0.0 53.5 jit_solution(3251101818255037770)
XLA Ops:
  0.6 0.0 copy-start
  0.6 0.0 copy-start.1
  0.6 2.1 %copy.7 = bf16[512,8,256]{2,0,1:T(8,128)(2,1)S(1)} copy(bf16[512,8,256]{2,1,0:T(8,128)(2,1)} %param.4) | data formatting | bytes 4194304 | tf_op args[1]
  2.7 0.0 copy-done
  2.7 0.0 copy-done.1
  2.7 49.2 %shard_map.50 = (bf16[256,512]{1,0:T(8,128)(2,1)S(1)}, f32[64,8,256]{2,1,0:T(8,128)S(1)}) custom-call(bf16[256,512]{1,0:T(8,128)(2,1)S(1)} %bitcast.7, bf16[8,512,256]{2,1,0:T(8,128)(2,1)S(1)} %bitcast.6, bf16[256,512]{1,0:T(8,128)(2,1)S(1)} %bitcast.8), custom_call_target="tpu_custom_call" | custom-call | tf_op jit(solution)/shard_map/pallas_call | solution.py:510
  52.0 0.7 %copy.10 = bf16[1,256,512]{2,1,0:T(8,128)(2,1)} copy(bf16[1,256,512]{2,1,0:T(8,128)(2,1)S(1)} %bitcast.9) | data formatting | bytes 524288
  52.7 0.8 %copy.11 = f32[64,8,256]{2,1,0:T(8,128)} copy(f32[64,8,256]{2,1,0:T(8,128)S(1)} %get-tuple-element.9) | data formatting | bytes 1048576
Async XLA Ops:
  0.6 2.1 %copy-start = (bf16[1,256,512]{2,1,0:T(8,128)(2,1)S(1)}, bf16[1,256,512]{2,1,0:T(8,128)(2,1)}, u32[]{:S(2)}) copy-start(bf16[1,256,512]{2,1,0:T(8,128)(2,1)} %param.3) | copy-start | bytes 786436
  0.6 2.1 %copy-start.1 = (bf16[1,256,512]{2,1,0:T(8,128)(2,1)S(1)}, bf16[1,256,512]{2,1,0:T(8,128)(2,1)}, u32[]{:S(2)}) copy-start(bf16[1,256,512]{2,1,0:T(8,128)(2,1)} %param.5) | copy-start | bytes 786436

commit v3 on v2

--- a/solution.py
+++ b/solution.py
@@ -464,15 +464,15 @@
 
     turned = x_ref[...].T
     backward(0, grad_first, lambda: scatter_first(0, 2, mm(turned, grads_s[0, 2])))
+    scatter_second(1, 0)
+    scatter_second(1, 1)
     scatter_first(0, 0, mm(turned, grads_s[0, 0]))
     scatter_first(0, 1, mm(turned, grads_s[0, 1]))
+    scatter_second(0, 3)
     for which in range(2):
         fsend[which] = input_grad(0, which).astype(BF16)
     full = head_copy(2, fsend, frecv)
     full.start()
-    scatter_second(1, 0)
-    scatter_second(1, 1)
-    scatter_second(0, 3)
     scatter_second(0, 2)
     full.wait_recv()
     for which in range(2):

time: 53.7 us -> 53 us (0.987)
  Pallas kernels: 49.2 us -> 48.6 us
    pallas_call x1, Pallas kernels: 49.2 us -> 48.6 us  [fused_call(): pl.pallas_call(functools.partial(fused, n, scale), out_shape=(jax.ShapeDt...]
where the time goes in v3:
time: 53 us; the launch traced here: 52.9 us
  Pallas kernels  48.6 us (92%)
  local copies, waits for them, and re-layouts  3.58 us (7%)
  between operations  0.68 us (1%)
    pallas_call x1, Pallas kernels, fused_call(): pl.pallas_call(functools.partial(fused, n, scale), out_shape=(jax.ShapeDt...  48.6 us
    unnamed x7, local copies, waits for them, and re-layouts  3.58 us

profile of v3, /device:TPU:0, one launch (start us, length us, event | category | flops | bytes accessed | tf_op | source)
XLA Modules:
  0.0 52.9 jit_solution(18441010797504001766)
XLA Ops:
  0.6 0.0 copy-start
  0.6 0.0 copy-start.1
  0.6 2.1 %copy.7 = bf16[512,8,256]{2,0,1:T(8,128)(2,1)S(1)} copy(bf16[512,8,256]{2,1,0:T(8,128)(2,1)} %param.4) | data formatting | bytes 4194304 | tf_op args[1]
  2.7 0.0 copy-done
  2.7 0.0 copy-done.1
  2.7 48.6 %shard_map.50 = (bf16[256,512]{1,0:T(8,128)(2,1)S(1)}, f32[64,8,256]{2,1,0:T(8,128)S(1)}) custom-call(bf16[256,512]{1,0:T(8,128)(2,1)S(1)} %bitcast.7, bf16[8,512,256]{2,1,0:T(8,128)(2,1)S(1)} %bitcast.6, bf16[256,512]{1,0:T(8,128)(2,1)S(1)} %bitcast.8), custom_call_target="tpu_custom_call" | custom-call | tf_op jit(solution)/shard_map/pallas_call | solution.py:510
  51.4 0.7 %copy.10 = bf16[1,256,512]{2,1,0:T(8,128)(2,1)} copy(bf16[1,256,512]{2,1,0:T(8,128)(2,1)S(1)} %bitcast.9) | data formatting | bytes 524288
  52.1 0.8 %copy.11 = f32[64,8,256]{2,1,0:T(8,128)} copy(f32[64,8,256]{2,1,0:T(8,128)S(1)} %get-tuple-element.9) | data formatting | bytes 1048576
Async XLA Ops:
  0.6 2.1 %copy-start = (bf16[1,256,512]{2,1,0:T(8,128)(2,1)S(1)}, bf16[1,256,512]{2,1,0:T(8,128)(2,1)}, u32[]{:S(2)}) copy-start(bf16[1,256,512]{2,1,0:T(8,128)(2,1)} %param.3) | copy-start | bytes 786436
  0.6 2.1 %copy-start.1 = (bf16[1,256,512]{2,1,0:T(8,128)(2,1)S(1)}, bf16[1,256,512]{2,1,0:T(8,128)(2,1)}, u32[]{:S(2)}) copy-start(bf16[1,256,512]{2,1,0:T(8,128)(2,1)} %param.5) | copy-start | bytes 786436
